TPU v7x, 32 devices: a whole 2x2x4 slice. The times are simulated.
32 devices in a mesh: pair: 16 (over z, y, core), irrep: 2 (over x).
Axes of the slice: x: 2, y: 2, z: 4, core: 2. Of those that a mesh axis runs over, the one named last changes fastest.
Arguments:
- blocks: bfloat16 [16, 2, 1280, 1280], P(None, 'irrep', 'pair'), may hold values from -6 to 6
- coefficients: bfloat16 [1280, 2048], P(None, 'irrep'), may hold values from -0.15625 to 0.15625
- shell_batch_functions: int32 [1280], replicated, may hold values from 0 to 1279, each once
- irrep_counts: int32 [8], replicated, may hold values from 128 to 256, as said below
- pair_symmetry: int32 [16, 2], P('pair', 'irrep'), may hold values from 0 to 7
Outputs:
- orbital_pair_integrals: float32 [16, 2, 8, 256, 256], P('pair', 'irrep')
Inputs may be any that keep to these rules, and one draw needn't show every extreme that they name: `shell_batch_functions`: each AO function appears exactly once. `irrep_counts`: irrep 0 holds all 256 virtual orbitals.
All inputs are finite; a program needn't handle non-finite values.
Results may differ from a plain program's by a relative error of at most 0.0029.
Values may be sent and summed in bfloat16 or wider, within the bound.
A program may use at most 128 MiB of HBM per device.

v0:
```python
import jax
import jax.numpy as jnp
from jax import lax
from jax.sharding import PartitionSpec as P

NAO = 1280
VIR = 256
NIRR = 8


def mask_columns(whole, irrep_counts):
    width = whole.shape[1]
    col = jnp.arange(width, dtype=jnp.int32)
    owner = col // VIR
    irrep_labels = jnp.arange(irrep_counts.shape[0], dtype=jnp.int32)
    limit = jnp.sum(
        jnp.where(owner[:, None] == irrep_labels[None, :], irrep_counts[None, :], 0), axis=1
    )
    live = col % VIR < limit
    return jnp.where(live[None, :], whole, jnp.zeros_like(whole))


def finish_pairs(moved, third_row_group, symmetry):

    def one_pair(half, sym_value):
        half_three = half.reshape(half.shape[0], NIRR, VIR)
        partner_irrep = jnp.bitwise_xor(jnp.arange(NIRR, dtype=jnp.int32), sym_value)
        selected_option = jnp.take(half_three, partner_irrep, axis=1)
        return jnp.einsum(
            "ytq,ytj->tqj", third_row_group, selected_option, preferred_element_type=jnp.float32
        )

    return jax.vmap(one_pair)(moved, symmetry)


def body(blocks, coefficients, shell_batch_functions, irrep_counts, pair_symmetry):
    pairs_here = blocks.shape[0]
    batch_rows = blocks.shape[2]
    whole = lax.all_gather(coefficients, "irrep", axis=1, tiled=True)
    masked = mask_columns(whole, irrep_counts)
    third_row_group = jnp.take(masked, shell_batch_functions, axis=0).reshape(NAO, NIRR, VIR)
    gathered = lax.all_to_all(
        blocks.reshape(pairs_here, batch_rows, NAO), "pair", split_axis=0, concat_axis=1, tiled=True
    )
    local_pair_list = gathered.shape[0]
    moved = jnp.dot(
        gathered.reshape(local_pair_list * NAO, NAO), masked, preferred_element_type=jnp.float32
    ).astype(jnp.bfloat16)
    moved = moved.reshape(local_pair_list, NAO, NIRR * VIR)
    result = finish_pairs(moved, third_row_group, pair_symmetry[:, 0])
    return result[:, None]


def solution(mesh):
    in_specs = (P(None, "irrep", "pair", None), P(None, "irrep"), P(), P(), P("pair", "irrep"))
    out_specs = P("pair", "irrep", None, None, None)
    return jax.shard_map(body, mesh=mesh, in_specs=in_specs, out_specs=out_specs, check_vma=False)
```

profile of v0, /device:TPU:0, one launch (start us, length us, event | category | flops | bytes accessed | tf_op | source)
XLA Modules:
  0.0 145.2 jit_solution(13259157394186770481)
XLA Ops:
  6.5 0.0 copy-start
  6.5 0.0 copy-start.1
  6.5 0.0 all-gather.2.cloned.1.call-start
  6.5 0.7 all-gather.2.cloned.1.call-update
  7.3 7.4 %all-to-all-start = ((bf16[16,80,1280]{2,1,0:T(8,128)(2,1)}), bf16[16,80,1280]{2,1,0:T(8,128)(2,1)S(1)}, u32[]{:S(2)}, u32[]{:S(2)}) async-start(bf16[16,80,1280]{2,1,0:T(8,128)(2,1)} %bitcast.24), calls=%async_computation | async-start | bytes 6553600 | tf_op jit(solution)/shard_map/all_to_all | solution.py:42
  15.4 0.0 copy-done
  15.4 0.0 copy-done.1
  15.4 0.1 select_reduce_fusion
  15.5 64.7 %all-gather.2.cloned.1.call-done = bf16[1280,2048]{1,0:T(8,128)(2,1)} async-done(((bf16[1280,1024]{1,0:T(8,128)(2,1)}), bf16[1280,2048]{1,0:T(8,128)(2,1)}) %all-gather.2.cloned.1.call-update) | async-done | bytes 5242896 | tf_op jit(solution)/shard_map/all_gather | solution.py:39
  80.2 5.2 %broadcast_select_fusion = bf16[1280,2048]{1,0:T(8,128)(2,1)} fusion(bf16[1280,2048]{1,0:T(8,128)(2,1)} %all-gather.2.cloned.1.call-done, pred[2048]{0:T(1024)(128)(4,1)S(1)} %fusion.13), kind=kLoop, calls=%fused_computation.8 | loop fusion | flops 2621440 | bytes 10487808 | tf_op jit(solution)/shard_map/jit(_where)/select_n | solution.py:20
  85.4 14.0 %gather_fusion = bf16[1280,2048]{1,0:T(8,128)(2,1)} fusion(bf16[1280,2048]{1,0:T(8,128)(2,1)} %broadcast_select_fusion, s32[2048]{0:T(1024)S(1)} %pad_clamp_fusion), kind=kCustom, calls=%fused_computation | custom fusion | bytes 10490880 | tf_op jit(solution)/shard_map/jit(_take)/gather | solution.py:41
  99.4 7.9 %copy.11 = bf16[1280,2048]{0,1:T(8,128)(2,1)} copy(bf16[1280,2048]{1,0:T(8,128)(2,1)} %gather_fusion) | data formatting | bytes 10485760 | tf_op jit(solution)/shard_map/jit(_take)/gather | solution.py:41
  107.2 0.0 all-to-all-done
  107.2 10.5 %convolution_convert_fusion = bf16[2048,1280]{1,0:T(8,128)(2,1)} fusion(bf16[1280,2048]{1,0:T(8,128)(2,1)} %broadcast_select_fusion, bf16[1280,1280]{1,0:T(8,128)(2,1)S(1)} %bitcast.25), kind=kOutput, calls=%fused_computation.2 | convolution fusion | flops 6713507840 | bytes 13762560 | tf_op jit(solution)/shard_map/dot_general | solution.py:46
  117.7 7.8 %copy.10 = bf16[1,1280,8,256]{3,1,2,0:T(8,128)(2,1)} copy(bf16[1,1280,8,256]{1,3,2,0:T(8,128)(2,1)} %bitcast.23) | data formatting | bytes 10485760 | tf_op jit(solution)/shard_map/vmap()/reshape;reshape | solution.py:26
  125.5 5.7 %gather_fusion.1 = bf16[8,1280,256]{2,1,0:T(8,128)(2,1)} fusion(bf16[1,1280,8,256]{3,1,2,0:T(8,128)(2,1)} %copy.10, s32[8]{0:T(128)S(1)} %or_bitcast_fusion), kind=kCustom, calls=%fused_computation.1 | custom fusion | bytes 10485824 | tf_op jit(solution)/shard_map/vmap(jit(_take))/gather | solution.py:28
  131.2 7.1 %fusion.8 = f32[1,1,8,256,256]{4,3,2,1,0:T(8,128)} fusion(bf16[8,1280,256]{2,1,0:T(8,128)(2,1)} %gather_fusion.1, pred[8]{0:T(512)(128)(4,1)S(1)} %compare_and_fusion.1, bf16[1280,8,256]{0,2,1:T(8,128)(2,1)} %bitcast.22, pred[1280]{0:T(1024)(128)(4,1)S(1)} %compare_and_fusion), kind=kOutput, calls=%fused_computation.12 | convolution fusion | flops 1347420160 | bytes 12584200 | tf_op jit(solution)/shard_map/vmap(ytq,ytj->tqj)/dot_general | solution.py:29
  (9 shorter events, 0.1 us)
Async XLA Ops:
  6.5 8.8 %copy-start = (s32[1280]{0:T(1024)S(1)}, s32[1280]{0:T(1024)}, u32[]{:S(2)}) copy-start(s32[1280]{0:T(1024)} %param.7) | copy-start | bytes 15364
  6.5 8.9 %copy-start.1 = (s32[8]{0:T(128)S(1)}, s32[8]{0:T(128)}, u32[]{:S(2)}) copy-start(s32[8]{0:T(128)} %param.8) | copy-start | bytes 100
  6.5 73.7 %all-gather.2.cloned.1.call-start = ((), (), s32[]{:S(2)}) async-start(), calls=%async_computation.1 | async-start | bytes 7864320 | tf_op jit(solution)/shard_map/all_gather | solution.py:39
  7.3 100.0 %all-to-all-start = ((bf16[16,80,1280]{2,1,0:T(8,128)(2,1)}), bf16[16,80,1280]{2,1,0:T(8,128)(2,1)S(1)}, u32[]{:S(2)}, u32[]{:S(2)}) async-start(bf16[16,80,1280]{2,1,0:T(8,128)(2,1)} %bitcast.24), calls=%async_computation | async-start | bytes 6553600 | tf_op jit(solution)/shard_map/all_to_all | solution.py:42
Sparse Core Ops, SparseCore 0:
  8.9 71.2 all-gather.1
where the time goes:
time: 146 us; the launch traced here: 145 us
  waiting for transfers between devices  65.4 us (45%)
  local copies, waits for them, and re-layouts  35.4 us (24%)
  matrix products  17.5 us (12%)
  between operations  14.1 us (10%)
  starting transfers between devices  7.4 us (5%)
  other arithmetic  5.3 us (4%)
    all_gather x1, waiting for transfers between devices, body(): whole = lax.all_gather(coefficients, 'irrep', axis=1, tiled=True)  64.7 us
    gather x2, local copies, waits for them, and re-layouts, body(): jnp.take(masked, shell_batch_functions, axis=0).reshape(NAO, NIRR, VIR)  21.9 us
    dot_general x1, matrix products, body(): jnp.dot(gathered.reshape(local_pair_list * NAO, NAO), masked, preferred_e...  10.5 us
    another operation x1, local copies, waits for them, and re-layouts, one_pair(): half_three = half.reshape(half.shape[0], NIRR, VIR)  7.81 us
    all_to_all x1, starting transfers between devices, body(): lax.all_to_all(blocks.reshape(pairs_here, batch_rows, NAO), 'pair', split...  7.4 us
    dot_general x1, matrix products, one_pair(): jnp.einsum('ytq,ytj->tqj', third_row_group, selected_option, preferred_el...  7.1 us
    gather x2, local copies, waits for them, and re-layouts, one_pair(): selected_option = jnp.take(half_three, partner_irrep, axis=1)  5.74 us
    select_n x1, other arithmetic, mask_columns(): return jnp.where(live[None, :], whole, jnp.zeros_like(whole))  5.15 us
  transfers between devices with their start and end apart: 2, of which 1 were waited for; matrix products, arithmetic and copies ran while one was open for 19% of the time, Pallas kernels for 0%

commit v1 on v0

--- a/solution.py
+++ b/solution.py
@@ -36,7 +36,15 @@
 def body(blocks, coefficients, shell_batch_functions, irrep_counts, pair_symmetry):
     pairs_here = blocks.shape[0]
     batch_rows = blocks.shape[2]
-    whole = lax.all_gather(coefficients, "irrep", axis=1, tiled=True)
+    ways, here, step = (lax.axis_size("irrep"), lax.axis_index("irrep"), coefficients.shape[1])
+    line, have = (coefficients, 1)
+    while have < ways:
+        line = jnp.concatenate(
+            [line, lax.ppermute(line, "irrep", [(d, (d - have) % ways) for d in range(ways)])],
+            axis=1,
+        )
+        have = 2 * have
+    whole = jnp.roll(line, here * step, axis=1)
     masked = mask_columns(whole, irrep_counts)
     third_row_group = jnp.take(masked, shell_batch_functions, axis=0).reshape(NAO, NIRR, VIR)
     gathered = lax.all_to_all(

time: 146 us -> 129 us (0.88)
  between operations: 14.1 us -> 0.75 us
  waiting for transfers between devices: 65.4 us -> 57.1 us
  other arithmetic: 5.3 us -> 8.01 us
  starting transfers between devices: 7.4 us -> 9.07 us
    all_gather x1 -> x0, waiting for transfers between devices: 64.7 us -> none  [body(): whole = lax.all_gather(coefficients, 'irrep', axis=1, tiled=True)]
    ppermute x0 -> x1, waiting for transfers between devices: none -> 57.1 us  [body(): lax.ppermute(line, 'irrep', [(d, (d - have) % ways) for d in range(ways)])]
    select_n x1, other arithmetic: 5.15 us -> 7.87 us  [mask_columns(): return jnp.where(live[None, :], whole, jnp.zeros_like(whole))]
    ppermute x0 -> x1, starting transfers between devices: none -> 1.56 us  [body(): lax.ppermute(line, 'irrep', [(d, (d - have) % ways) for d in range(ways)])]
  transfers between devices with their start and end apart: 2 -> 2, of which waited for: 1 -> 1; matrix products, arithmetic and copies ran while one was open for 19% -> 23% of each run, Pallas kernels for 0% -> 0%
where the time goes in v1:
time: 129 us; the launch traced here: 128 us
  waiting for transfers between devices  57.1 us (44%)
  local copies, waits for them, and re-layouts  35.5 us (28%)
  matrix products  17.5 us (14%)
  starting transfers between devices  9.07 us (7%)
  other arithmetic  8.01 us (6%)
    ppermute x1, waiting for transfers between devices, body(): lax.ppermute(line, 'irrep', [(d, (d - have) % ways) for d in range(ways)])  57.1 us
    gather x2, local copies, waits for them, and re-layouts, body(): jnp.take(masked, shell_batch_functions, axis=0).reshape(NAO, NIRR, VIR)  21.9 us
    dot_general x1, matrix products, body(): jnp.dot(gathered.reshape(local_pair_list * NAO, NAO), masked, preferred_e...  10.5 us
    select_n x1, other arithmetic, mask_columns(): return jnp.where(live[None, :], whole, jnp.zeros_like(whole))  7.87 us
    another operation x1, local copies, waits for them, and re-layouts, one_pair(): half_three = half.reshape(half.shape[0], NIRR, VIR)  7.82 us
    all_to_all x1, starting transfers between devices, body(): lax.all_to_all(blocks.reshape(pairs_here, batch_rows, NAO), 'pair', split...  7.52 us
    dot_general x1, matrix products, one_pair(): jnp.einsum('ytq,ytj->tqj', third_row_group, selected_option, preferred_el...  7.09 us
    gather x2, local copies, waits for them, and re-layouts, one_pair(): selected_option = jnp.take(half_three, partner_irrep, axis=1)  5.75 us
  transfers between devices with their start and end apart: 2, of which 1 were waited for; matrix products, arithmetic and copies ran while one was open for 23% of the time, Pallas kernels for 0%

profile of v1, /device:TPU:0, one launch (start us, length us, event | category | flops | bytes accessed | tf_op | source)
XLA Modules:
  0.0 127.9 jit_solution(4134434346488018877)
XLA Ops:
  0.0 0.0 copy-start
  0.0 0.0 copy-start.1
  0.0 7.5 %all-to-all-start = ((bf16[16,80,1280]{2,1,0:T(8,128)(2,1)}), bf16[16,80,1280]{2,1,0:T(8,128)(2,1)S(1)}, u32[]{:S(2)}, u32[]{:S(2)}) async-start(bf16[16,80,1280]{2,1,0:T(8,128)(2,1)} %bitcast.24), calls=%async_computation | async-start | bytes 6553600 | tf_op jit(solution)/shard_map/all_to_all | solution.py:50
  7.5 1.6 %collective-permute-start = (bf16[1280,1024]{1,0:T(8,128)(2,1)}, bf16[1280,1024]{1,0:T(8,128)(2,1)}, u32[]{:S(2)}, u32[]{:S(2)}) collective-permute-start(bf16[1280,1024]{1,0:T(8,128)(2,1)} %param.6), channel_id=1, source_target_pairs={{0,1},{1,0},{2,3},{3,2},{4,5},{5,4},{6,7},{7,6},{8,9},{9,8},{10,11... | collective-permute-start | bytes 7864328 | tf_op jit(solution)/shard_map/ppermute | solution.py:43
  9.8 0.0 copy-done
  9.8 0.0 copy-done.1
  9.8 0.1 select_reduce_fusion
  10.0 57.1 %collective-permute-done = bf16[1280,1024]{1,0:T(8,128)(2,1)} collective-permute-done((bf16[1280,1024]{1,0:T(8,128)(2,1)}, bf16[1280,1024]{1,0:T(8,128)(2,1)}, u32[]{:S(2)}, u32[]{:S(2)}) %collective-permute-start) | collective-permute-done | bytes 2621472 | tf_op jit(solution)/shard_map/ppermute | solution.py:43
  67.0 7.9 %fusion.3 = bf16[1280,2048]{1,0:T(8,128)(2,1)} fusion(s32[]{:T(128)S(6)} %select_n.86, bf16[1280,1024]{1,0:T(8,128)(2,1)} %param.6, bf16[1280,1024]{1,0:T(8,128)(2,1)} %collective-permute-done, pred[2048]{0:T(1024)(128)(4,1)S(1)} %fusion.17), kind=kLoop, calls=%fused_computation.10 | loop fusion | flops 23592960 | bytes 10487812 | tf_op jit(solution)/shard_map/jit(_where)/select_n | solution.py:20
  74.9 14.0 %gather_fusion = bf16[1280,2048]{1,0:T(8,128)(2,1)} fusion(bf16[1280,2048]{1,0:T(8,128)(2,1)} %fusion.3, s32[2048]{0:T(1024)S(1)} %pad_clamp_fusion), kind=kCustom, calls=%fused_computation | custom fusion | bytes 10490880 | tf_op jit(solution)/shard_map/jit(_take)/gather | solution.py:49
  88.9 7.9 %copy.11 = bf16[1280,2048]{0,1:T(8,128)(2,1)} copy(bf16[1280,2048]{1,0:T(8,128)(2,1)} %gather_fusion) | data formatting | bytes 10485760 | tf_op jit(solution)/shard_map/jit(_take)/gather | solution.py:49
  96.8 0.0 all-to-all-done
  96.8 10.5 %convolution_convert_fusion = bf16[2048,1280]{1,0:T(8,128)(2,1)} fusion(bf16[1280,2048]{1,0:T(8,128)(2,1)} %fusion.3, bf16[1280,1280]{1,0:T(8,128)(2,1)S(1)} %bitcast.25), kind=kOutput, calls=%fused_computation.6 | convolution fusion | flops 6713507840 | bytes 13762560 | tf_op jit(solution)/shard_map/dot_general | solution.py:54
  107.3 7.8 %copy.10 = bf16[1,1280,8,256]{3,1,2,0:T(8,128)(2,1)} copy(bf16[1,1280,8,256]{1,3,2,0:T(8,128)(2,1)} %bitcast.23) | data formatting | bytes 10485760 | tf_op jit(solution)/shard_map/vmap()/reshape;reshape | solution.py:26
  115.1 5.7 %gather_fusion.1 = bf16[8,1280,256]{2,1,0:T(8,128)(2,1)} fusion(bf16[1,1280,8,256]{3,1,2,0:T(8,128)(2,1)} %copy.10, s32[8]{0:T(128)S(1)} %or_bitcast_fusion), kind=kCustom, calls=%fused_computation.1 | custom fusion | bytes 10485824 | tf_op jit(solution)/shard_map/vmap(jit(_take))/gather | solution.py:28
  120.8 7.1 %fusion.12 = f32[1,1,8,256,256]{4,3,2,1,0:T(8,128)} fusion(bf16[8,1280,256]{2,1,0:T(8,128)(2,1)} %gather_fusion.1, pred[8]{0:T(512)(128)(4,1)S(1)} %compare_and_fusion.1, bf16[1280,8,256]{0,2,1:T(8,128)(2,1)} %bitcast.22, pred[1280]{0:T(1024)(128)(4,1)S(1)} %compare_and_fusion), kind=kOutput, calls=%fused_computation.19 | convolution fusion | flops 1347420160 | bytes 12584200 | tf_op jit(solution)/shard_map/vmap(ytq,ytj->tqj)/dot_general | solution.py:29
  (9 shorter events, 0.1 us)
Async XLA Ops:
  0.0 9.8 %copy-start = (s32[1280]{0:T(1024)S(1)}, s32[1280]{0:T(1024)}, u32[]{:S(2)}) copy-start(s32[1280]{0:T(1024)} %param.7) | copy-start | bytes 15364
  0.0 9.8 %copy-start.1 = (s32[8]{0:T(128)S(1)}, s32[8]{0:T(128)}, u32[]{:S(2)}) copy-start(s32[8]{0:T(128)} %param.8) | copy-start | bytes 100
  0.0 96.8 %all-to-all-start = ((bf16[16,80,1280]{2,1,0:T(8,128)(2,1)}), bf16[16,80,1280]{2,1,0:T(8,128)(2,1)S(1)}, u32[]{:S(2)}, u32[]{:S(2)}) async-start(bf16[16,80,1280]{2,1,0:T(8,128)(2,1)} %bitcast.24), calls=%async_computation | async-start | bytes 6553600 | tf_op jit(solution)/shard_map/all_to_all | solution.py:50
  7.5 59.5 %collective-permute-start = (bf16[1280,1024]{1,0:T(8,128)(2,1)}, bf16[1280,1024]{1,0:T(8,128)(2,1)}, u32[]{:S(2)}, u32[]{:S(2)}) collective-permute-start(bf16[1280,1024]{1,0:T(8,128)(2,1)} %param.6), channel_id=1, source_target_pairs={{0,1},{1,0},{2,3},{3,2},{4,5},{5,4},{6,7},{7,6},{8,9},{9,8},{10,11... | collective-permute-start | bytes 7864328 | tf_op jit(solution)/shard_map/ppermute | solution.py:43
